TPU v7x, 512 devices: a whole 4x4x16 slice. The times are simulated.
512 devices in a mesh: grp: 16 (over y, z_hi), mem: 32 (over z_lo, x, core).
Axes of the slice: x: 4, y: 4, z: 16 (z_hi: 4, z_lo: 4; z = z_hi * 4 + z_lo), core: 2. Of those that a mesh axis runs over, the one named last changes fastest.
Arguments:
- activations: bfloat16 [2, 65536, 512], P(None, ('grp', 'mem'))
- out_grads: bfloat16 [2, 65536, 512], P(None, ('grp', 'mem'))
- inverse_slots: float32 [2, 2, 8192, 512], P(None, None, ('grp', 'mem')), as said below
- gradient: float32 [2, 512, 512], replicated, may hold values from -6 to 6
- owners: int32 [2, 2], replicated, may hold values from 0 to 15
- counts: int32 [512], replicated, may hold values from 32 to 128, as said below
Outputs:
- factor_slots: float32 [2, 2, 8192, 512], P(None, None, ('grp', 'mem'))
- preconditioned: float32 [2, 512, 512], P(None, 'mem', 'grp')
Inputs may be any that keep to these rules, and one draw needn't show every extreme that they name: `counts`: live tokens of a device; some device has all 128 live in every draw. `inverse_slots`: symmetric in every slot.
All inputs are finite; a program needn't handle non-finite values.
Results may differ from a plain program's by a relative error of at most 0.0003.
Values sent between devices are 32-bit elements; how exact they have to be, the bound alone decides.
A program may use at most 64 MiB of HBM per device.

v0:
```python
import jax
import jax.numpy as jnp
from jax import lax
from jax.sharding import PartitionSpec as P

damping = 0.1


def broadcast(value, axis, source):
    kept = jnp.where(lax.axis_index(axis) == source, value, 0).astype(value.dtype)
    return lax.psum(kept, axis)


def masked_terms(rows, live_count):
    place = lax.broadcasted_iota(jnp.int32, (rows.shape[0], 1), 0)
    masked = jnp.where(place < live_count, rows, jnp.zeros_like(rows))
    return lax.dot_general(
        masked, rows, (((0,), (0,)), ((), ())), preferred_element_type=jnp.float32
    )


def body(activations, out_grads, inverse_slots, gradient, owners, counts):
    highest = lax.Precision.HIGHEST
    layer_count = activations.shape[0]
    width = activations.shape[2]
    row_share = inverse_slots.shape[2]
    col_share = width // lax.axis_size("grp")
    group_index = lax.axis_index("grp")
    device_index = group_index * lax.axis_size("mem") + lax.axis_index("mem")
    live_count = lax.dynamic_slice_in_dim(counts, device_index, 1, 0)[0]
    all_tokens = jnp.sum(counts).astype(jnp.float32)
    term_list = []
    for layer in range(layer_count):
        for source in (activations, out_grads):
            term_list.append(masked_terms(source[layer], live_count))
    terms = jnp.stack(term_list).reshape(layer_count, 2, width, width)
    offset = lax.axis_index("mem") * row_share
    summed = lax.psum(terms, ("grp", "mem"))
    full_factor = summed / all_tokens + damping * jnp.eye(width, dtype=jnp.float32)
    own_rows = lax.dynamic_slice_in_dim(full_factor, offset, row_share, 2)
    stale_full = lax.all_gather(inverse_slots, "mem", axis=2, tiled=True)
    product = jnp.einsum("abrk,abkj->abrj", inverse_slots, full_factor, precision=highest)
    refreshed_rows = 2.0 * inverse_slots - jnp.einsum(
        "abrk,abkj->abrj", product, stale_full, precision=highest
    )
    shared_rows = []
    for layer in range(layer_count):
        for side in range(2):
            shared_rows.append(broadcast(refreshed_rows[layer, side], "grp", owners[layer, side]))
    shared = jnp.stack(shared_rows).reshape(layer_count, 2, row_share, width)
    left_side = jnp.einsum("arj,ajk->ark", shared[:, 1], gradient, precision=highest)
    col_start = group_index * col_share
    own_piece = lax.dynamic_slice_in_dim(
        lax.all_gather(shared[:, 0], "mem", axis=1, tiled=True), col_start, col_share, 2
    )
    preconditioned = jnp.einsum("ark,akj->arj", left_side, own_piece, precision=highest)
    factor_slots = jnp.where(
        (owners == group_index)[:, :, None, None], own_rows, jnp.zeros_like(own_rows)
    )
    return (factor_slots, preconditioned)


def solution(mesh):
    placed = (
        P(None, ("grp", "mem"), None),
        P(None, ("grp", "mem"), None),
        P(None, None, ("grp", "mem"), None),
        P(),
        P(),
        P(),
    )
    return jax.shard_map(
        body,
        mesh=mesh,
        in_specs=placed,
        out_specs=(P(None, None, ("grp", "mem"), None), P(None, "mem", "grp")),
        check_vma=False,
    )
```

profile of v0, /device:TPU:1, one launch (start us, length us, event | category | flops | bytes accessed | tf_op | source)
XLA Modules:
  0.0 799.3 jit_solution(10877795697490555595)
XLA Ops:
  8.0 0.0 all-reduce.4.cloned.1.call-start
  8.1 1.4 dynamic_slice.9
  9.5 0.6 iota_compare_fusion.1
  10.1 1.4 convolution_bitcast_fusion
  11.5 1.4 convolution_bitcast_fusion.2
  12.9 1.4 convolution_bitcast_fusion.1
  14.2 1.4 convolution_bitcast_fusion.3
  15.6 2.4 pad_maximum_fusion
  18.0 0.0 all-reduce.4.cloned.1.call-update
  18.0 0.0 all-gather.4.cloned.1.call-start
  18.1 0.5 all-gather.4.cloned.1.call-update
  18.6 0.0 all-reduce.6.cloned.1.call-start
  18.7 0.0 copy-done.4
  18.7 0.6 reduce_sum.9
  20.0 0.6 fusion.38
  23.2 0.1 fusion
  23.3 488.3 %all-reduce.4.cloned.1.call-done = f32[2,2,512,512]{3,2,1,0:T(8,128)} async-done(((f32[2,2,512,512]{3,2,1,0:T(8,128)}), f32[2,2,512,512]{3,2,1,0:T(8,128)}) %all-reduce.4.cloned.1.call-update) | async-done | bytes 4194320 | tf_op jit(solution)/shard_map/psum | solution.py:38
  511.5 2.9 divide_add_fusion
  514.5 1.9 copy-done.1
  516.4 2.3 fusion.39
  518.7 4.3 convolution_subtract_fusion
  523.0 0.7 fusion.32
  523.7 0.0 all-reduce.6.cloned.1.call-update
  523.7 0.0 all-gather.6.cloned.1.call-start
  523.7 193.4 %all-reduce.6.cloned.1.call-done = (f32[1,16,512]{2,1,0:T(8,128)}, f32[1,16,512]{2,1,0:T(8,128)}, f32[1,16,512]{2,1,0:T(8,128)}, f32[1,16,512]{2,1,0:T(8,128)}) async-done(((f32[1,16,512]{2,1,0:T(8,128)}, f32[1,16,512]{2,1,0:T(8,128)}, f32[1,16,512]{2,1,0:T(8,128)}, f32[1,16,512]{2,1,0:T(8,128)}), (f32[1,16,512]{2,1,0:T(8,128)}, f32[1,16,512]{2,1,0:T(8,128)}, f32[1,16,512]{2,1,0:T(8,128)}, ...) | async-done | bytes 131088 | tf_op jit(solution)/shard_map/psum | solution.py:11
  717.1 0.8 pad_maximum_fusion.1
  717.9 0.6 slice.61
  718.6 0.0 all-gather.6.cloned.1.call-update
  718.6 1.6 dynamic-slice_select_fusion
  720.3 1.1 fusion.24
  721.4 68.3 %all-gather.6.cloned.1.call-done = f32[2,1,512,512]{3,2,1,0:T(8,128)} async-done(((f32[2,1,16,512]{3,2,1,0:T(8,128)}), f32[2,1,512,512]{3,2,1,0:T(8,128)}) %all-gather.6.cloned.1.call-update) | async-done | bytes 2097168 | tf_op jit(solution)/shard_map/all_gather | solution.py:54
  789.7 2.1 fusion.1
  (10 shorter events, 0.0 us)
Async XLA Ops:
  8.0 712.3 %copy-start = (f32[2,512,512]{2,1,0:T(8,128)S(1)}, f32[2,512,512]{2,1,0:T(8,128)}, u32[]{:S(2)}) copy-start(f32[2,512,512]{2,1,0:T(8,128)} %param.9) | copy-start | bytes 6291460
  8.0 503.5 %all-reduce.4.cloned.1.call-start = ((), (), s32[]{:S(2)}) async-start(), calls=%async_computation | async-start | bytes 8388608 | tf_op jit(solution)/shard_map/psum | solution.py:38
  18.0 0.7 copy-start.4
  18.0 2.0 copy-start.3
  18.0 500.7 %all-gather.4.cloned.1.call-start = ((), (), s32[]{:S(2)}) async-start(), calls=%async_computation.1 | async-start | bytes 4325376 | tf_op jit(solution)/shard_map/all_gather | solution.py:41
  18.6 698.5 %all-reduce.6.cloned.1.call-start = ((), (), s32[]{:S(2)}) async-start(), calls=%async_computation.3 | async-start | bytes 262144 | tf_op jit(solution)/shard_map/psum | solution.py:11
  23.3 493.1 %copy-start.2 = (f32[2,2,16,512]{3,2,1,0:T(8,128)S(1)}, f32[2,2,16,512]{3,2,1,0:T(8,128)}, u32[]{:S(2)}) copy-start(f32[2,2,16,512]{3,2,1,0:T(8,128)} %param.8) | copy-start | bytes 393220
  514.4 2.0 copy-start.1
  523.7 266.0 %all-gather.6.cloned.1.call-start = ((), (), s32[]{:S(2)}) async-start(), calls=%async_computation.2 | async-start | bytes 2162688 | tf_op jit(solution)/shard_map/all_gather | solution.py:54
Sparse Core Ops, SparseCore 0:
  18.2 493.3 all-reduce.3
  523.8 193.2 all-reduce.5
Sparse Core Ops, SparseCore 1:
  20.7 74.4 all-gather.3
  718.7 71.0 all-gather.5
where the time goes:
time: 800 us; the launch traced here: 799 us
  waiting for transfers between devices  751 us (94%)
  between operations  18.8 us (2%)
  matrix products  15.3 us (2%)
  other arithmetic  9.81 us (1%)
    psum x1, waiting for transfers between devices, body(): summed = lax.psum(terms, ('grp', 'mem'))  488 us
    psum x1, waiting for transfers between devices, broadcast(): return lax.psum(kept, axis)  193 us
    all_gather x1, waiting for transfers between devices, body(): lax.all_gather(shared[:, 0], 'mem', axis=1, tiled=True)  68.3 us
  transfers between devices with their start and end apart: 4, of which 3 were waited for; matrix products, arithmetic and copies ran while one was open for 1% of the time, Pallas kernels for 0%

commit v1 on v0

v1 whole, which is shorter than its diff:
```python
import jax
import jax.numpy as jnp
from jax import lax
from jax.experimental import pallas as pl
from jax.experimental.pallas import tpu as pltpu
from jax.sharding import PartitionSpec as P

MESH = pl.DeviceIdType.MESH
damping = 0.1
BLOCK_AT = (0, 4, 7, 9)


def device(x, y, z, c):
    return (y * 4 + z // 4, (z % 4) * 8 + x * 2 + c)


def high(a, b, dims=(((1,), (0,)), ((), ()))):
    return lax.dot_general(
        a, b, dims, precision=lax.Precision.HIGHEST, preferred_element_type=jnp.float32
    )


def kernel(
    owners, counts, acts, grads, slots, gradient,
    slots_out, pre_out,
    xin, inv, gmat, xsend, xrecv, xcat, terms, near, chunk, near2, part,
    zsend, zrecv, ztenth, zgath, piece, stack, full,
    vmsg, vnear, vown, vcore, vboth, vfar, vpart, vcols, vfull, rows_in, newrows, partner, pblock, pin, fin,
    lsem, xss, xrs, s1, q1, s2, q2, s3, q3, s4, q4, s5, q5,
    sv1, qv1, sv2, qv2, sv3, qv3, sv4, qv4, sf, qf, sr, qr, sp, qp,
):
    grp = lax.axis_index("grp")
    mem = lax.axis_index("mem")
    y = grp // 4
    z = (grp % 4) * 4 + mem // 8
    x = (mem // 2) % 4
    c = mem % 2
    zlo = z % 4
    zhi = z // 4
    layer = z % 2
    zpair = z + 1 - 2 * layer

    def remote(src, dst, ssem, rsem, target):
        return pltpu.make_async_remote_copy(
            src_ref=src, dst_ref=dst, send_sem=ssem, recv_sem=rsem, device_id=target, device_id_type=MESH
        )

    loads = [
        pltpu.make_async_copy(slots, inv, lsem.at[0]),
        pltpu.make_async_copy(acts, xin.at[0], lsem.at[1]),
        pltpu.make_async_copy(grads, xin.at[1], lsem.at[2]),
        pltpu.make_async_copy(gradient.at[layer], gmat, lsem.at[3]),
    ]
    for load in loads:
        load.start()

    core_peer = device(x, y, z, 1 - c)
    plane_peers = [
        (device((x + i) % 4, (y + j) % 4, z, c)) for i in range(4) for j in range(4) if i or j
    ]
    z_peers = [device(x, y, (z + i) % 16, c) for i in range(1, 16)]
    cross_peer = device(x, y, zpair, 1 - c)
    pair_peer = device(x, y, zpair, c)
    barrier = pltpu.get_barrier_semaphore()
    peers = [core_peer, cross_peer] + plane_peers + z_peers
    for peer in peers:
        pl.semaphore_signal(barrier, inc=1, device_id=peer, device_id_type=MESH)

    live = counts[grp * 32 + mem]

    def add(i, totals):
        return tuple(t + counts[i * 8 + k] for k, t in enumerate(totals))

    totals = lax.fori_loop(0, 64, add, (jnp.int32(0),) * 8)
    total = sum(totals[1:], totals[0])
    scale = 1.0 / (jnp.zeros((1, 128), jnp.float32) + total.astype(jnp.float32))

    loads[0].wait()
    for l in range(2):
        for s in range(2):
            mask = jnp.where(owners[l, s] == grp, 1.0, 0.0).astype(jnp.float32)
            for k in range(4):
                vmsg[k, s, l] = inv[l, s, :, 128 * k : 128 * k + 128] * mask
    loads[1].wait()
    loads[2].wait()
    keep = lax.broadcasted_iota(jnp.int32, (128, 512), 0) < live
    for l in range(2):
        xsend[l] = jnp.where(keep, xin[1 - c, l].astype(jnp.float32), 0.0)
        xcat[l, 0:128] = jnp.where(keep, xin[c, l].astype(jnp.float32), 0.0).astype(jnp.bfloat16)
    loads[3].wait()

    pl.semaphore_wait(barrier, len(peers))

    xcopies = [remote(xsend.at[l], xrecv.at[l], xss.at[l], xrs.at[l], core_peer) for l in range(2)]
    for copy in xcopies:
        copy.start()
    v1 = [
        remote(vmsg.at[(y + i) % 4], vnear.at[i - 1], sv1.at[i - 1], qv1.at[i - 1], device(x, (y + i) % 4, z, c))
        for i in range(1, 4)
    ]
    for copy in v1:
        copy.start()

    ring = (
        (x, device((x + 1) % 4, y, z, c), device((x + 3) % 4, y, z, c)),
        (y, device(x, (y + 1) % 4, z, c), device(x, (y + 3) % 4, z, c)),
    )

    def half(l, index, which):
        return pl.ds(pl.multiple_of((index % 4) * 320 + which * 160, 32), 160)

    def send1(l, d, k, index, which):
        copy = remote(
            terms.at[l, half(l, index, which)],
            near.at[l, d, k],
            s1.at[l * 6 + d * 3 + k],
            q1.at[l * 6 + d * 3 + k],
            ring[l][1 + d],
        )
        copy.start()
        return copy

    first = [None, None]
    for l in range(2):
        xcopies[l].wait()
        xcat[l, 128:256] = xrecv[l].astype(jnp.bfloat16)
        for i in range(4):
            block = lax.dot_general(
                xcat[l, :, 128 * i : 128 * i + 128],
                xcat[l, :, 128 * i : 512],
                (((0,), (0,)), ((), ())),
                preferred_element_type=jnp.float32,
            )
            for j in range(4 - i):
                at = (BLOCK_AT[i] + j) * 128
                terms[l, at : at + 128] = block[:, 128 * j : 128 * j + 128]
        p = ring[l][0]
        first[l] = [
            send1(l, 0, 0, p + 2, 0),
            send1(l, 1, 0, p + 2, 1),
            send1(l, 0, 1, p + 1, 1),
            send1(l, 1, 1, p + 3, 0),
        ]

    for copy in v1:
        copy.wait()
    for s in range(2):
        vown[s] = vmsg[y, s] + vnear[0, s] + vnear[1, s] + vnear[2, s]
    v2 = remote(vown.at[1 - c], vcore, sv2.at[0], qv2.at[0], core_peer)
    v2.start()

    for l in range(2):
        p = ring[l][0]
        for d in range(2):
            first[l][d].wait()
            to = half(l, p + (1 if d == 0 else 3), d)
            terms[l, to] = terms[l, to] + near[l, d, 0]
            first[l].append(send1(l, d, 2, p + (1 if d == 0 else 3), d))

    v2.wait()
    for l in range(2):
        vboth[l, c] = vown[c, l]
        vboth[l, 1 - c] = vcore[l]
    v3 = [
        remote(vboth.at[(z + i) % 2], vfar.at[i - 1], sv3.at[i - 1], qv3.at[i - 1], z_peers[i - 1])
        for i in range(1, 16)
    ]
    for copy in v3:
        copy.start()

    second = [[], []]
    for l in range(2):
        for copy in first[l][2:]:
            copy.wait()
        p = ring[l][0]
        chunk[l, 0:160] = terms[l, half(l, p, 0)] + near[l, 0, 2] + near[l, 1, 1]
        chunk[l, 160:320] = terms[l, half(l, p, 1)] + near[l, 0, 1] + near[l, 1, 2]
        q = ring[1 - l][0]
        for i in range(1, 4):
            to = (q + i) % 4
            target = device(x, to, z, c) if l == 0 else device(to, y, z, c)
            copy = remote(
                chunk.at[l, pl.ds(pl.multiple_of(to * 80, 16), 80)],
                near2.at[l, i - 1],
                s2.at[l * 3 + i - 1],
                q2.at[l * 3 + i - 1],
                target,
            )
            copy.start()
            second[l].append(copy)
    for l in range(2):
        for copy in second[l]:
            copy.wait()
        q = ring[1 - l][0]
        part[l] = (
            chunk[l, pl.ds(pl.multiple_of(q * 80, 16), 80)] + near2[l, 0] + near2[l, 1] + near2[l, 2]
        )
    for k in range(16):
        zsend[k] = part[k % 2, 10 * (k // 2) : 10 * (k // 2) + 10]
    third = [
        remote(zsend.at[(z + i) % 16], zrecv.at[i - 1], s3.at[i - 1], q3.at[i - 1], z_peers[i - 1])
        for i in range(1, 16)
    ]
    for i in (8, 7, 9, 6, 10, 5, 11, 4, 12, 3, 13, 2, 14, 1, 15):
        third[i - 1].start()

    for copy in v3:
        copy.wait()
    for r in range(4):
        got = vboth[layer] if r == 0 else vfar[r - 1]
        for i in range(r + 4, 16, 4):
            got = got + vfar[i - 1]
        vpart[(zlo + 4 - r) % 4] = got
    vcols[y, :, x] = vpart[...]
    v4 = [
        remote(vpart, vcols.at[y, :, x], sv4.at[k], qv4.at[k], plane_peers[k]) for k in range(15)
    ]
    for copy in v4:
        copy.start()

    for copy in third:
        copy.wait()
    tenth = zsend[z]
    for i in range(15):
        tenth = tenth + zrecv[i]
    ztenth[...] = tenth * scale
    zgath[z // 2] = ztenth[...]
    fourth = [
        remote(ztenth, zgath.at[z // 2], s4.at[i // 2 - 1], q4.at[i // 2 - 1], z_peers[i - 1])
        for i in range(2, 16, 2)
    ]
    for k in (3, 2, 4, 1, 5, 0, 6):
        fourth[k].start()
    for copy in fourth:
        copy.wait()
    for j in range(8):
        piece[10 * j : 10 * j + 10] = zgath[j]
    mine = jnp.where(layer == 0, x * 4 + y, y * 4 + x)
    at = pl.ds(pl.multiple_of(mine * 80, 16), 80)
    stack[at] = piece[...]
    fifth = [remote(piece, stack.at[at], s5.at[k], q5.at[k], plane_peers[k]) for k in range(15)]
    for copy in fifth:
        copy.start()

    for copy in v4:
        copy.wait()
    for k in range(4):
        vfull[:, 128 * k : 128 * k + 128] = vcols[k].reshape(512, 128)
    row_a = jnp.where(c == 1, (zlo // 2 * 2) * 4 + x, y * 4 + zhi)
    row_b = jnp.where(c == 1, (zlo // 2 * 2 + 1) * 4 + x, y * 4 + zhi)
    rows_in[0:32] = vfull[pl.ds(pl.multiple_of(row_a * 32, 32), 32)]
    rows_in[32:64] = vfull[pl.ds(pl.multiple_of(row_b * 32, 32), 32)]

    for copy in fifth:
        copy.wait()
    diagonal = jnp.where(
        lax.broadcasted_iota(jnp.int32, (128, 128), 0) == lax.broadcasted_iota(jnp.int32, (128, 128), 1),
        damping,
        0.0,
    ).astype(jnp.float32)
    for i in range(4):
        for j in range(i, 4):
            b = (BLOCK_AT[i] + j - i) * 128
            block = stack[b : b + 128]
            if i == j:
                full[128 * i : 128 * i + 128, 128 * j : 128 * j + 128] = block + diagonal
            else:
                full[128 * i : 128 * i + 128, 128 * j : 128 * j + 128] = block
                full[128 * j : 128 * j + 128, 128 * i : 128 * i + 128] = block.T

    def rows_of(plane_lo, core):
        return pl.ds(pl.multiple_of(plane_lo * 128 + x * 32 + core * 16, 16), 16)

    pair_lo = zpair % 4
    fcopies = [
        remote(full.at[rows_of(zlo, 1 - c)], fin.at[layer, c], sf.at[0], qf.at[0], core_peer),
        remote(full.at[rows_of(pair_lo, c)], fin.at[layer, c], sf.at[1], qf.at[1], pair_peer),
        remote(full.at[rows_of(pair_lo, 1 - c)], fin.at[layer, c], sf.at[2], qf.at[2], cross_peer),
    ]
    for copy in fcopies:
        copy.start()
    fin[layer, c] = full[rows_of(zlo, c)]

    half_way = high(rows_in[...], full[...])
    newrows[...] = 2.0 * rows_in[...] - high(half_way, vfull[...])

    rcopy = remote(newrows.at[0:32], partner, sr.at[0], qr.at[0], core_peer)

    @pl.when(c == 0)
    def _():
        rcopy.start()

    targets = [device(x, y, z, 0), device(x, y, zpair, 0), device(x, y, zpair, 1)]
    order = [(layer, 0), (1 - layer, 0), (1 - layer, 1)]
    pcopies = [
        remote(pblock.at[a * 2 + b], pin.at[layer], sp.at[k], qp.at[layer], targets[k])
        for k, (a, b) in enumerate(order)
    ]

    @pl.when(c == 1)
    def _():
        left = high(newrows[...], gmat[...])
        rcopy.wait_recv()
        result = high(left, partner[...], (((1,), (1,)), ((), ())))
        for k in range(4):
            pblock[k] = result[16 * k : 16 * k + 16]
        pin[layer] = pblock[layer * 2 + 1]
        for copy in pcopies:
            copy.start()

    for copy in fcopies:
        copy.wait()
    for l in range(2):
        for s in range(2):
            keep_slot = jnp.where(owners[l, s] == grp, 1.0, 0.0).astype(jnp.float32)
            slots_out[l, s] = fin[l, s] * keep_slot

    @pl.when(c == 0)
    def _():
        rcopy.wait_send()
        remote(pblock.at[0], pin.at[layer], sp.at[0], qp.at[layer], core_peer).wait_recv()

    @pl.when(c == 1)
    def _():
        for copy in pcopies:
            copy.wait_send()

    remote(pblock.at[0], pin.at[1 - layer], sp.at[0], qp.at[1 - layer], core_peer).wait_recv()
    pre_out[...] = pin[...]


def body(activations, out_grads, inverse_slots, gradient, owners, counts):
    f32, bf16 = jnp.float32, jnp.bfloat16
    anywhere = pl.BlockSpec(memory_space=pl.ANY)
    scalars = pl.BlockSpec(memory_space=pltpu.SMEM)
    whole = pl.BlockSpec(memory_space=pltpu.VMEM)
    vm = lambda *shape: pltpu.VMEM(shape, f32)
    dma = lambda n: pltpu.SemaphoreType.DMA((n,))
    return pl.pallas_call(
        kernel,
        out_shape=(
            jax.ShapeDtypeStruct((2, 2, 16, 512), f32),
            jax.ShapeDtypeStruct((2, 16, 32), f32),
        ),
        in_specs=[scalars, scalars, anywhere, anywhere, anywhere, anywhere],
        out_specs=(whole, whole),
        scratch_shapes=[
            pltpu.VMEM((2, 2, 128, 512), bf16),
            vm(2, 2, 16, 512),
            vm(512, 512),
            vm(2, 128, 512),
            vm(2, 128, 512),
            pltpu.VMEM((2, 256, 512), bf16),
            vm(2, 1280, 128),
            vm(2, 2, 3, 160, 128),
            vm(2, 320, 128),
            vm(2, 3, 80, 128),
            vm(2, 80, 128),
            vm(16, 10, 128),
            vm(15, 10, 128),
            vm(10, 128),
            vm(8, 10, 128),
            vm(80, 128),
            vm(1280, 128),
            vm(512, 512),
            vm(4, 2, 2, 16, 128),
            vm(3, 2, 2, 16, 128),
            vm(2, 2, 16, 128),
            vm(2, 16, 128),
            vm(2, 2, 16, 128),
            vm(15, 2, 16, 128),
            vm(4, 2, 16, 128),
            vm(4, 4, 4, 2, 16, 128),
            vm(512, 512),
            vm(64, 512),
            vm(64, 512),
            vm(32, 512),
            vm(4, 16, 32),
            vm(2, 16, 32),
            vm(2, 2, 16, 512),
            dma(4), dma(2), dma(2), dma(12), dma(12), dma(6), dma(6), dma(15), dma(15), dma(7), dma(7),
            dma(15), dma(15),
            dma(3), dma(3), dma(1), dma(1), dma(15), dma(15), dma(15), dma(15), dma(3), dma(3),
            dma(1), dma(1), dma(3), dma(2),
        ],
        compiler_params=pltpu.CompilerParams(
            collective_id=0, has_side_effects=True, vmem_limit_bytes=40 * 1024 * 1024
        ),
    )(owners, counts, activations, out_grads, inverse_slots, gradient)


def solution(mesh):
    placed = (
        P(None, ("grp", "mem"), None),
        P(None, ("grp", "mem"), None),
        P(None, None, ("grp", "mem"), None),
        P(),
        P(),
        P(),
    )
    return jax.shard_map(
        body,
        mesh=mesh,
        in_specs=placed,
        out_specs=(P(None, None, ("grp", "mem"), None), P(None, "mem", "grp")),
        check_vma=False,
    )
```

time: 800 us -> 74.2 us (0.09)
  waiting for transfers between devices: 751 us -> 0 us
  Pallas kernels: 0 us -> 66.3 us
  between operations: 18.8 us -> 0.65 us
  matrix products: 15.3 us -> 0 us
  other arithmetic: 9.81 us -> 0 us
    psum x2 -> x0, waiting for transfers between devices: 682 us -> none  [the longest x1 488 us: body(): summed = lax.psum(terms, ('grp', 'mem'))]
    all_gather x2 -> x0, waiting for transfers between devices: 68.3 us -> none  [the longest x1 68.3 us: body(): lax.all_gather(shared[:, 0], 'mem', axis=1, tiled=True)]
    pallas_call x0 -> x1, Pallas kernels: none -> 66.3 us  [body(): pl.pallas_call(kernel, out_shape=(jax.ShapeDtypeStruct((2, 2, 16, 512), f...]
    dot_general x8 -> x0, matrix products: 15.3 us -> none  [the longest x4 5.47 us: masked_terms(): lax.dot_general(masked, rows, (((0,), (0,)), ((), ())), preferred_element...]
  transfers between devices with their start and end apart: 4 -> 0, of which waited for: 3 -> 0; matrix products, arithmetic and copies ran while one was open for 1% -> 0% of each run, Pallas kernels for 0% -> 0%
where the time goes in v1:
time: 74.2 us; the launch traced here: 74 us
  Pallas kernels  66.3 us (89%)
  local copies, waits for them, and re-layouts  7.01 us (9%)
    pallas_call x1, Pallas kernels, body(): pl.pallas_call(kernel, out_shape=(jax.ShapeDtypeStruct((2, 2, 16, 512), f...  66.3 us
    unnamed x14, local copies, waits for them, and re-layouts  7.01 us

profile of v1, /device:TPU:1, one launch (start us, length us, event | category | flops | bytes accessed | tf_op | source)
XLA Modules:
  0.0 74.0 jit_solution(4985622505434511405)
XLA Ops:
  0.6 0.0 copy-start
  0.6 1.6 %copy-done = f32[2,512,512]{2,1,0:T(8,128)S(1)} copy-done((f32[2,512,512]{2,1,0:T(8,128)S(1)}, f32[2,512,512]{2,1,0:T(8,128)}, u32[]{:S(2)}) %copy-start) | copy-done | bytes 2097176
  2.2 0.0 copy-start.1
  2.2 0.9 %copy-done.1 = bf16[2,128,512]{2,1,0:T(8,128)(2,1)S(1)} copy-done((bf16[2,128,512]{2,1,0:T(8,128)(2,1)S(1)}, bf16[2,128,512]{2,1,0:T(8,128)(2,1)}, u32[]{:S(2)}) %copy-start.1) | copy-done | bytes 262168
  3.2 0.0 copy-start.2
  3.2 0.9 %copy-done.2 = bf16[2,128,512]{2,1,0:T(8,128)(2,1)S(1)} copy-done((bf16[2,128,512]{2,1,0:T(8,128)(2,1)S(1)}, bf16[2,128,512]{2,1,0:T(8,128)(2,1)}, u32[]{:S(2)}) %copy-start.2) | copy-done | bytes 262168
  4.1 0.0 copy-start.3
  4.1 0.9 %copy-done.3 = f32[2,2,16,512]{3,2,1,0:T(8,128)S(1)} copy-done((f32[2,2,16,512]{3,2,1,0:T(8,128)S(1)}, f32[2,2,16,512]{3,2,1,0:T(8,128)}, u32[]{:S(2)}) %copy-start.3) | copy-done | bytes 131096
  5.0 0.0 copy-start.4
  5.0 0.7 copy-done.4
  5.7 0.0 copy-start.5
  5.7 0.7 copy-done.5
  6.4 66.3 %shard_map.77 = (f32[2,2,16,512]{3,2,1,0:T(8,128)S(1)}, f32[2,16,32]{2,1,0:T(8,128)S(1)}) custom-call(s32[2,2]{1,0:T(2,128)S(1)} %copy-done.5, s32[512]{0:T(512)S(1)} %copy-done.4, bf16[2,128,512]{2,1,0:T(8,128)(2,1)S(1)} %copy-done.1, bf16[2,128,512]{2,1,0:T(8,128)(2,1)S(1)} %copy-done.2, f32[2,2,16,512]{3,2,1,0:T(8,128)S(1)} %copy-done.3, ...), custom_call_target="tpu_custom_call" | custom-call | tf_op jit(solution)/shard_map/pallas_call | solution.py:339
  72.7 0.7 copy.10
  73.3 0.6 copy.11
Async XLA Ops:
  0.6 1.6 %copy-start = (f32[2,512,512]{2,1,0:T(8,128)S(1)}, f32[2,512,512]{2,1,0:T(8,128)}, u32[]{:S(2)}) copy-start(f32[2,512,512]{2,1,0:T(8,128)} %gradient.1) | copy-start | bytes 6291460
  2.2 0.9 %copy-start.1 = (bf16[2,128,512]{2,1,0:T(8,128)(2,1)S(1)}, bf16[2,128,512]{2,1,0:T(8,128)(2,1)}, u32[]{:S(2)}) copy-start(bf16[2,128,512]{2,1,0:T(8,128)(2,1)} %acts.1) | copy-start | bytes 786436
  3.2 0.9 %copy-start.2 = (bf16[2,128,512]{2,1,0:T(8,128)(2,1)S(1)}, bf16[2,128,512]{2,1,0:T(8,128)(2,1)}, u32[]{:S(2)}) copy-start(bf16[2,128,512]{2,1,0:T(8,128)(2,1)} %grads.1) | copy-start | bytes 786436
  4.1 0.9 %copy-start.3 = (f32[2,2,16,512]{3,2,1,0:T(8,128)S(1)}, f32[2,2,16,512]{3,2,1,0:T(8,128)}, u32[]{:S(2)}) copy-start(f32[2,2,16,512]{3,2,1,0:T(8,128)} %slots.1) | copy-start | bytes 393220
  5.0 0.7 copy-start.4
  5.7 0.7 copy-start.5

commit v2 on v1

v2 whole, which is shorter than its diff:
```python
import jax
import jax.numpy as jnp
from jax import lax
from jax.experimental import pallas as pl
from jax.experimental.pallas import tpu as pltpu
from jax.sharding import PartitionSpec as P

MESH = pl.DeviceIdType.MESH
damping = 0.1


def device(x, y, z, c):
    return (y * 4 + z // 4, (z % 4) * 8 + x * 2 + c)


def split(a):
    top = a.astype(jnp.bfloat16)
    return top, (a - top.astype(jnp.float32)).astype(jnp.bfloat16)


def three(a, b, dims=(((1,), (0,)), ((), ()))):
    one = lambda p, q: lax.dot_general(p, q, dims, preferred_element_type=jnp.float32)
    return one(a[0], b[0]) + (one(a[0], b[1]) + one(a[1], b[0]))


def high(a, b, dims=(((1,), (0,)), ((), ()))):
    return lax.dot_general(
        a, b, dims, precision=lax.Precision.HIGHEST, preferred_element_type=jnp.float32
    )


NEAR_FIRST = (2, 14, 4, 12, 6, 10, 8)
PAIRS = ((0, 1), (0, 2), (0, 3), (1, 2), (1, 3), (2, 3))


def in_half(a, b):
    return (b - a) % 4 < 2 or ((b - a) % 4 == 2 and a < 2)


def kernel(
    owners_in, counts_in, acts, grads, slots, gradient,
    slots_out, pre_out,
    owners, counts, xin, inv, gmat, xsend, xrecv, xcat, terms, near, chunk, near2, part,
    zrecv, unit, zgath, stack, ordered, full,
    vmsg, vnear, vown, vcore, vboth, vfar, vpart, vcols, vfull, rows_in, other_hi, other_lo, base,
    diag_own, diag_far, diag_sum, diag_x,
    newrows, partner, pblock, pin, fin,
    lsem, xss, xrs, s1, q1, s2, q2, s3, q3, s4, q4, s5, q5,
    sv1, qv1, sv2, qv2, sv3, qv3, sv4, qv4, se3, qe3, se4, qe4, sf, qf, sr, qr, sp, qp, ready,
):
    grp = lax.axis_index("grp")
    mem = lax.axis_index("mem")
    y = grp // 4
    z = (grp % 4) * 4 + mem // 8
    x = (mem // 2) % 4
    c = mem % 2
    zlo = z % 4
    zhi = z // 4
    layer = z % 2
    zpair = z + 1 - 2 * layer

    def remote(src, dst, ssem, rsem, target):
        return pltpu.make_async_remote_copy(
            src_ref=src, dst_ref=dst, send_sem=ssem, recv_sem=rsem, device_id=target, device_id_type=MESH
        )

    def signal(sem, peer):
        pl.semaphore_signal(sem, inc=1, device_id=peer, device_id_type=MESH)

    core_peer = device(x, y, z, 1 - c)
    x_peers = [device((x + i) % 4, y, z, c) for i in range(1, 4)]
    y_peers = [device(x, (y + i) % 4, z, c) for i in range(1, 4)]
    plane_shift = [(i, j) for i in range(4) for j in range(4) if i or j]
    plane_peers = [device((x + i) % 4, (y + j) % 4, z, c) for i, j in plane_shift]
    z_peers = [device(x, y, (z + i) % 16, c) for i in range(1, 16)]
    pair_peer = device(x, y, zpair, c)
    cross_peer = device(x, y, zpair, 1 - c)
    barrier = pltpu.get_barrier_semaphore()
    close = [core_peer] + x_peers + y_peers + [z_peers[i - 1] for i in (1, 2, 14, 15)]
    for peer in close:
        signal(barrier, peer)

    loads = [
        pltpu.make_async_copy(counts_in, counts, lsem.at[0]),
        pltpu.make_async_copy(acts, xin.at[0], lsem.at[1]),
        pltpu.make_async_copy(grads, xin.at[1], lsem.at[2]),
        pltpu.make_async_copy(owners_in, owners, lsem.at[3]),
        pltpu.make_async_copy(slots, inv, lsem.at[4]),
        pltpu.make_async_copy(gradient.at[layer], gmat, lsem.at[5]),
    ]
    for load in loads:
        load.start()

    for k in range(3):
        loads[k].wait()
    live = counts[grp * 32 + mem]
    keep = lax.broadcasted_iota(jnp.int32, (128, 512), 0) < live
    for l in range(2):
        theirs = jnp.where(keep, xin[1 - c, l].astype(jnp.float32), 0.0)
        xsend[l] = theirs
        ours = jnp.where(keep, xin[c, l].astype(jnp.float32), 0.0)
        xcat[l, 0:128] = ours.astype(jnp.bfloat16)
        for s, values in ((1 - c, theirs), (c, ours)):
            squares = jnp.sum(values * values, axis=0, keepdims=True)
            for k in range(4):
                vmsg[k, s, l, 16:17] = squares[:, 128:256]
                vmsg[k, s, l, 17:18] = squares[:, 384:512]
    loads[3].wait()
    loads[4].wait()
    for l in range(2):
        for s in range(2):
            mask = jnp.where(owners[l, s] == grp, 1.0, 0.0).astype(jnp.float32)
            for k in range(4):
                vmsg[k, s, l, 0:16] = inv[l, s, :, 128 * k : 128 * k + 128] * mask

    pl.semaphore_wait(barrier, len(close))

    xcopies = [remote(xsend.at[l], xrecv.at[l], xss.at[l], xrs.at[l], core_peer) for l in range(2)]
    for copy in xcopies:
        copy.start()
    signal(ready.at[0], z_peers[1])
    signal(ready.at[0], z_peers[13])
    v1 = [
        remote(vmsg.at[(y + i) % 4], vnear.at[i - 1], sv1.at[i - 1], qv1.at[i - 1], y_peers[i - 1])
        for i in range(1, 4)
    ]
    for copy in v1:
        copy.start()

    where = (x, y)
    across = (x_peers, y_peers)
    at_or_above = lax.broadcasted_iota(jnp.int32, (128, 128), 0) <= lax.broadcasted_iota(
        jnp.int32, (128, 128), 1
    )
    first = [[], []]
    for l in range(2):
        xcopies[l].wait()
        xcat[l, 128:256] = xrecv[l].astype(jnp.bfloat16)
        corner = []
        for i in range(4):
            block = lax.dot_general(
                xcat[l, :, 128 * i : 128 * i + 128],
                xcat[l, :, 128 * i : 512],
                (((0,), (0,)), ((), ())),
                preferred_element_type=jnp.float32,
            )
            corner.append(block[:, 0:128])
            for j in range(i + 1, 4):
                at = 256 + PAIRS.index((i, j)) * 128
                terms[l, at : at + 128] = block[:, 128 * (j - i) : 128 * (j - i) + 128]
        terms[l, 0:128] = jnp.where(at_or_above, corner[0], corner[1])
        terms[l, 128:256] = jnp.where(at_or_above, corner[2], corner[3])
        for i in range(1, 4):
            to = (where[l] + i) % 4
            copy = remote(
                terms.at[l, pl.ds(pl.multiple_of(to * 256, 256), 256)],
                near.at[l, i - 1],
                s1.at[l * 3 + i - 1],
                q1.at[l * 3 + i - 1],
                across[l][i - 1],
            )
            copy.start()
            first[l].append(copy)

    pl.semaphore_wait(ready.at[0], 2)
    signal(ready.at[1], z_peers[3])
    signal(ready.at[1], z_peers[11])

    for copy in v1:
        copy.wait()
    for s in range(2):
        vown[s] = vmsg[y, s] + vnear[0, s] + vnear[1, s] + vnear[2, s]
    v2 = remote(vown.at[1 - c], vcore, sv2.at[0], qv2.at[0], core_peer)
    v2.start()

    def add(i, totals):
        return tuple(t + counts[i * 8 + k] for k, t in enumerate(totals))

    totals = lax.fori_loop(0, 64, add, (jnp.int32(0),) * 8)
    total = sum(totals[1:], totals[0])
    scale = 1.0 / (jnp.zeros((1, 128), jnp.float32) + total.astype(jnp.float32))

    v2.wait()
    for l in range(2):
        vboth[l, c] = vown[c, l, 0:16]
        vboth[l, 1 - c] = vcore[l, 0:16]
        diag_own[l] = vown[c, l, 16:18] + vcore[l, 16:18]
    pl.semaphore_wait(ready.at[1], 2)
    far_first = (8, 7, 9, 6, 10, 5, 11, 4, 12, 3, 13, 2, 14, 1, 15)
    v3 = [
        remote(vboth.at[(z + i) % 2], vfar.at[i - 1], sv3.at[i - 1], qv3.at[i - 1], z_peers[i - 1])
        for i in range(1, 16)
    ]
    e3 = [
        remote(diag_own.at[(z + i) % 2], diag_far.at[i - 1], se3.at[i - 1], qe3.at[i - 1], z_peers[i - 1])
        for i in range(1, 16)
    ]

    def kept(step):
        row = (zlo + 4 - step) % 4
        turn = (y - row + 4) % 4
        return (turn < 2) | ((turn == 2) & (row < 2))

    @pl.when(kept(0))
    def _():
        for i in far_first:
            v3[i - 1].start()

    for i in far_first:
        e3[i - 1].start()

    second = [[], []]
    for l in range(2):
        for copy in first[l]:
            copy.wait()
        own = pl.ds(pl.multiple_of(where[l] * 256, 256), 256)
        chunk[l] = terms[l, own] + near[l, 0] + near[l, 1] + near[l, 2]
        for i in range(1, 4):
            to = (where[1 - l] + i) % 4
            copy = remote(
                chunk.at[l, pl.ds(pl.multiple_of(to * 64, 64), 64)],
                near2.at[l, i - 1],
                s2.at[l * 3 + i - 1],
                q2.at[l * 3 + i - 1],
                across[1 - l][i - 1],
            )
            copy.start()
            second[l].append(copy)
    for l in range(2):
        for copy in second[l]:
            copy.wait()
        own = pl.ds(pl.multiple_of(where[1 - l] * 64, 64), 64)
        part[l] = (chunk[l, own] + near2[l, 0] + near2[l, 1] + near2[l, 2]).reshape(8, 8, 128)
    third = [
        remote(
            part.at[(z + i) % 2, (z + i) % 16 // 2], zrecv.at[i - 1], s3.at[i - 1], q3.at[i - 1], z_peers[i - 1]
        )
        for i in range(1, 16)
    ]
    for i in far_first:
        third[i - 1].start()

    @pl.when(kept(0))
    def _():
        for copy in v3:
            copy.wait_send()

    for r in range(4):

        @pl.when(kept(r))
        def _():
            got = vboth[layer] if r == 0 else None
            for i in range(r or 4, 16, 4):
                v3[i - 1].wait_recv()
                got = vfar[i - 1] if got is None else got + vfar[i - 1]
            vpart[(zlo + 4 - r) % 4] = got

    v4 = []
    for d in range(3):
        row = (y + 4 - d) % 4
        v4.append(
            [
                remote(
                    vpart.at[row], vcols.at[y, row, x], sv4.at[d * 15 + k], qv4.at[d * 15 + k], plane_peers[k]
                )
                for k in range(15)
            ]
        )
    for d in range(2):
        row = (y + 4 - d) % 4
        vcols[y, row, x] = vpart[row]
        for copy in v4[d]:
            copy.start()

    @pl.when(y >= 2)
    def _():
        row = (y + 2) % 4
        vcols[y, row, x] = vpart[row]
        for copy in v4[2]:
            copy.start()

    got = diag_own[layer]
    for i in range(15):
        e3[i].wait()
        got = got + diag_far[i]
    diag_sum[...] = got
    e4 = [remote(diag_sum, diag_x.at[i], se4.at[i], qe4.at[i], x_peers[i]) for i in range(3)]
    for copy in e4:
        copy.start()

    for copy in third:
        copy.wait()
    got = part[layer, z // 2]
    for i in range(15):
        got = got + zrecv[i]
    unit[...] = got * scale
    zgath[0] = unit[...]
    fourth = {
        i: remote(unit, zgath.at[k + 1], s4.at[k], q4.at[k], z_peers[i - 1])
        for k, i in enumerate(NEAR_FIRST)
    }
    for i in (8, 6, 10, 4, 12, 2, 14):
        fourth[i].start()
    mine = jnp.where(layer == 0, x * 4 + y, y * 4 + x)
    fifth = []
    for lo, hi in ((0, 3), (3, 7), (7, 8)):
        for i in NEAR_FIRST[max(lo, 1) - 1 : hi - 1]:
            fourth[i].wait_recv()
        for k in range(15):
            at = len(fifth)
            fifth.append(
                remote(zgath.at[lo:hi], stack.at[mine, lo:hi], s5.at[at], q5.at[at], plane_peers[k])
            )
            fifth[at].start()
    stack[mine] = zgath[...]

    for k, (i, j) in enumerate(plane_shift):
        v4[0][k].wait()
        v4[1][k].wait()

        @pl.when((y + 4 - j) % 4 >= 2)
        def _():
            v4[2][k].wait_recv()

        @pl.when(y >= 2)
        def _():
            v4[2][k].wait_send()

    for a in range(4):
        for b in range(4):
            block = vcols[b, a].reshape(128, 128) if in_half(a, b) else vcols[a, b].reshape(128, 128).T
            vfull[128 * a : 128 * a + 128, 128 * b : 128 * b + 128] = block
    row_a = jnp.where(c == 1, (zlo // 2 * 2) * 4 + x, y * 4 + zhi)
    row_b = jnp.where(c == 1, (zlo // 2 * 2 + 1) * 4 + x, y * 4 + zhi)
    rows_in[0:32] = vfull[pl.ds(pl.multiple_of(row_a * 32, 32), 32)]
    rows_in[32:64] = vfull[pl.ds(pl.multiple_of(row_b * 32, 32), 32)]
    loads[5].wait()

    @pl.when(c == 0)
    def _():
        top, low = split(vfull[...])
        other_hi[...] = top
        other_lo[...] = low
        base[...] = 2.0 * rows_in[...]

    @pl.when(c == 1)
    def _():
        right = split(gmat[...])
        top, low = split(three(split(vfull[...]), right))
        other_hi[...] = top
        other_lo[...] = low
        base[...] = 2.0 * three(split(rows_in[...]), right)

    for copy in e4:
        copy.wait()
    second_diag = (diag_sum[...] + diag_x[0] + diag_x[1] + diag_x[2]) * scale

    for copy in fifth:
        copy.wait()
    for i in NEAR_FIRST:
        fourth[i].wait_send()
    for k, i in enumerate((0,) + NEAR_FIRST):
        at = (z + 16 - i) % 16 // 2
        for p in range(16):
            ordered[p, at] = stack[p, k]

    on_diag = lax.broadcasted_iota(jnp.int32, (128, 128), 0) == lax.broadcasted_iota(jnp.int32, (128, 128), 1)
    eye = jnp.where(on_diag, damping, 0.0).astype(jnp.float32)
    for k in range(2):
        both = ordered[2 * k : 2 * k + 2].reshape(128, 128)
        turned = both.T
        at = 256 * k
        full[at : at + 128, at : at + 128] = jnp.where(at_or_above, both, turned) + eye
        lower = jnp.where(at_or_above, turned, both)
        full[at + 128 : at + 256, at + 128 : at + 256] = (
            jnp.where(on_diag, second_diag[k : k + 1, :], lower) + eye
        )
    for k, (i, j) in enumerate(PAIRS):
        block = ordered[4 + 2 * k : 6 + 2 * k].reshape(128, 128)
        full[128 * i : 128 * i + 128, 128 * j : 128 * j + 128] = block
        full[128 * j : 128 * j + 128, 128 * i : 128 * i + 128] = block.T

    def rows_of(plane_lo, core):
        return pl.ds(pl.multiple_of(plane_lo * 128 + x * 32 + core * 16, 16), 16)

    pair_lo = zpair % 4
    fcopies = [
        remote(full.at[rows_of(zlo, 1 - c)], fin.at[layer, c], sf.at[0], qf.at[0], core_peer),
        remote(full.at[rows_of(pair_lo, c)], fin.at[layer, c], sf.at[1], qf.at[1], pair_peer),
        remote(full.at[rows_of(pair_lo, 1 - c)], fin.at[layer, c], sf.at[2], qf.at[2], cross_peer),
    ]
    for copy in fcopies:
        copy.start()
    fin[layer, c] = full[rows_of(zlo, c)]

    half_way = three(split(rows_in[...]), split(full[...]))
    newrows[...] = base[...] - three(split(half_way), (other_hi[...], other_lo[...]))

    rcopy = remote(newrows.at[0:32], partner, sr.at[0], qr.at[0], core_peer)

    @pl.when(c == 0)
    def _():
        rcopy.start()

    targets = [device(x, y, z, 0), device(x, y, zpair, 0), device(x, y, zpair, 1)]
    order = [(layer, 0), (1 - layer, 0), (1 - layer, 1)]
    pcopies = [
        remote(pblock.at[a * 2 + b], pin.at[layer], sp.at[k], qp.at[layer], targets[k])
        for k, (a, b) in enumerate(order)
    ]

    @pl.when(c == 1)
    def _():
        rcopy.wait_recv()
        result = high(newrows[...], partner[...], (((1,), (1,)), ((), ())))
        for k in range(4):
            pblock[k] = result[16 * k : 16 * k + 16]
        pin[layer] = pblock[layer * 2 + 1]
        for copy in pcopies:
            copy.start()

    for copy in fcopies:
        copy.wait()
    for l in range(2):
        for s in range(2):
            keep_slot = jnp.where(owners[l, s] == grp, 1.0, 0.0).astype(jnp.float32)
            slots_out[l, s] = fin[l, s] * keep_slot

    @pl.when(c == 0)
    def _():
        rcopy.wait_send()
        remote(pblock.at[0], pin.at[layer], sp.at[0], qp.at[layer], core_peer).wait_recv()

    @pl.when(c == 1)
    def _():
        for copy in pcopies:
            copy.wait_send()

    remote(pblock.at[0], pin.at[1 - layer], sp.at[0], qp.at[1 - layer], core_peer).wait_recv()
    pre_out[...] = pin[...]


def body(activations, out_grads, inverse_slots, gradient, owners, counts):
    f32, bf16 = jnp.float32, jnp.bfloat16
    whole = pl.BlockSpec(memory_space=pltpu.VMEM)
    vm = lambda *shape: pltpu.VMEM(shape, f32)
    dma = lambda n: pltpu.SemaphoreType.DMA((n,))
    return pl.pallas_call(
        kernel,
        out_shape=(
            jax.ShapeDtypeStruct((2, 2, 16, 512), f32),
            jax.ShapeDtypeStruct((2, 16, 32), f32),
        ),
        in_specs=[pl.BlockSpec(memory_space=pltpu.HBM)] * 6,
        out_specs=(whole, whole),
        scratch_shapes=[
            pltpu.SMEM((2, 2), jnp.int32),
            pltpu.SMEM((512,), jnp.int32),
            pltpu.VMEM((2, 2, 128, 512), bf16),
            vm(2, 2, 16, 512),
            vm(512, 512),
            vm(2, 128, 512),
            vm(2, 128, 512),
            pltpu.VMEM((2, 256, 512), bf16),
            vm(2, 1024, 128),
            vm(2, 3, 256, 128),
            vm(2, 256, 128),
            vm(2, 3, 64, 128),
            vm(2, 8, 8, 128),
            vm(15, 8, 128),
            vm(8, 128),
            vm(8, 8, 128),
            vm(16, 8, 8, 128),
            vm(16, 8, 8, 128),
            vm(512, 512),
            vm(4, 2, 2, 18, 128),
            vm(3, 2, 2, 18, 128),
            vm(2, 2, 18, 128),
            vm(2, 18, 128),
            vm(2, 2, 16, 128),
            vm(15, 2, 16, 128),
            vm(4, 2, 16, 128),
            vm(4, 4, 4, 2, 16, 128),
            vm(512, 512),
            vm(64, 512),
            pltpu.VMEM((512, 512), bf16),
            pltpu.VMEM((512, 512), bf16),
            vm(64, 512),
            vm(2, 2, 128),
            vm(15, 2, 128),
            vm(2, 128),
            vm(3, 2, 128),
            vm(64, 512),
            vm(32, 512),
            vm(4, 16, 32),
            vm(2, 16, 32),
            vm(2, 2, 16, 512),
            dma(6), dma(2), dma(2), dma(6), dma(6), dma(6), dma(6), dma(15), dma(15), dma(7), dma(7),
            dma(45), dma(45),
            dma(3), dma(3), dma(1), dma(1), dma(15), dma(15), dma(45), dma(45), dma(15), dma(15), dma(3), dma(3),
            dma(3), dma(3), dma(1), dma(1), dma(3), dma(2),
            pltpu.SemaphoreType.REGULAR((2,)),
        ],
        compiler_params=pltpu.CompilerParams(
            collective_id=0, has_side_effects=True, vmem_limit_bytes=62 * 1024 * 1024
        ),
    )(owners, counts, activations, out_grads, inverse_slots, gradient)


def solution(mesh):
    placed = (
        P(None, ("grp", "mem"), None),
        P(None, ("grp", "mem"), None),
        P(None, None, ("grp", "mem"), None),
        P(),
        P(),
        P(),
    )
    return jax.shard_map(
        body,
        mesh=mesh,
        in_specs=placed,
        out_specs=(P(None, None, ("grp", "mem"), None), P(None, "mem", "grp")),
        check_vma=False,
    )
```

time: 74.2 us -> 63.2 us (0.85)
  Pallas kernels: 66.3 us -> 59.4 us
  local copies, waits for them, and re-layouts: 7.01 us -> 2.89 us
    pallas_call x1, Pallas kernels: 66.3 us -> 59.4 us  [body(): pl.pallas_call(kernel, out_shape=(jax.ShapeDtypeStruct((2, 2, 16, 512), f...]
    unnamed x14 -> x2, local copies, waits for them, and re-layouts: 7.01 us -> 2.89 us
where the time goes in v2:
time: 63.2 us; the launch traced here: 62.9 us
  Pallas kernels  59.4 us (94%)
  local copies, waits for them, and re-layouts  2.89 us (5%)
  between operations  0.64 us (1%)
    pallas_call x1, Pallas kernels, body(): pl.pallas_call(kernel, out_shape=(jax.ShapeDtypeStruct((2, 2, 16, 512), f...  59.4 us
    unnamed x2, local copies, waits for them, and re-layouts  2.89 us

profile of v2, /device:TPU:1, one launch (start us, length us, event | category | flops | bytes accessed | tf_op | source)
XLA Modules:
  0.0 62.9 jit_solution(5572430614526126052)
XLA Ops:
  0.6 59.4 %shard_map.77 = (f32[2,2,16,512]{3,2,1,0:T(8,128)}, f32[2,16,32]{2,1,0:T(8,128)}) custom-call(s32[2,2]{1,0:T(2,128)} %owners_in.1, s32[512]{0:T(512)} %counts_in.1, bf16[2,128,512]{2,1,0:T(8,128)(2,1)} %acts.1, bf16[2,128,512]{2,1,0:T(8,128)(2,1)} %grads.1, f32[2,2,16,512]{3,2,1,0:T(8,128)} %slots.1, f32[2,512,512]{2,1,0:T(8,128)} %gradient.1), custom_call_target="tpu_custom_call" | custom-call | tf_op jit(solution)/shard_map/pallas_call | solution.py:448
  60.0 1.6 %copy.10 = f32[2,2,16,512]{3,2,1,0:T(8,128)} copy(f32[2,2,16,512]{3,2,1,0:T(8,128)} %get-tuple-element.4) | data formatting | bytes 262144
  61.6 1.3 %copy.11 = f32[2,16,32]{2,1,0:T(8,128)} copy(f32[2,16,32]{2,1,0:T(8,128)} %get-tuple-element.5) | data formatting | bytes 8192

commit v3 on v2

--- a/solution.py
+++ b/solution.py
@@ -21,12 +21,6 @@
 def three(a, b, dims=(((1,), (0,)), ((), ()))):
     one = lambda p, q: lax.dot_general(p, q, dims, preferred_element_type=jnp.float32)
     return one(a[0], b[0]) + (one(a[0], b[1]) + one(a[1], b[0]))
-
-
-def high(a, b, dims=(((1,), (0,)), ((), ()))):
-    return lax.dot_general(
-        a, b, dims, precision=lax.Precision.HIGHEST, preferred_element_type=jnp.float32
-    )
 
 
 NEAR_FIRST = (2, 14, 4, 12, 6, 10, 8)
@@ -70,13 +64,16 @@
     core_peer = device(x, y, z, 1 - c)
     x_peers = [device((x + i) % 4, y, z, c) for i in range(1, 4)]
     y_peers = [device(x, (y + i) % 4, z, c) for i in range(1, 4)]
-    plane_shift = [(i, j) for i in range(4) for j in range(4) if i or j]
+    plane_shift = sorted(
+        [(i, j) for i in range(4) for j in range(4) if i or j], key=lambda at: -(min(at[0], 4 - at[0]) + min(at[1], 4 - at[1]))
+    )
     plane_peers = [device((x + i) % 4, (y + j) % 4, z, c) for i, j in plane_shift]
     z_peers = [device(x, y, (z + i) % 16, c) for i in range(1, 16)]
     pair_peer = device(x, y, zpair, c)
     cross_peer = device(x, y, zpair, 1 - c)
     barrier = pltpu.get_barrier_semaphore()
-    close = [core_peer] + x_peers + y_peers + [z_peers[i - 1] for i in (1, 2, 14, 15)]
+    beside = [x_peers[0], x_peers[2], y_peers[0], y_peers[2], z_peers[0], z_peers[14]]
+    close = [core_peer] + beside
     for peer in close:
         signal(barrier, peer)
 
@@ -97,9 +94,9 @@
     keep = lax.broadcasted_iota(jnp.int32, (128, 512), 0) < live
     for l in range(2):
         theirs = jnp.where(keep, xin[1 - c, l].astype(jnp.float32), 0.0)
-        xsend[l] = theirs
+        xsend[l] = theirs.T
         ours = jnp.where(keep, xin[c, l].astype(jnp.float32), 0.0)
-        xcat[l, 0:128] = ours.astype(jnp.bfloat16)
+        xcat[l, :, 0:128] = ours.T.astype(jnp.bfloat16)
         for s, values in ((1 - c, theirs), (c, ours)):
             squares = jnp.sum(values * values, axis=0, keepdims=True)
             for k in range(4):
@@ -118,14 +115,12 @@
     xcopies = [remote(xsend.at[l], xrecv.at[l], xss.at[l], xrs.at[l], core_peer) for l in range(2)]
     for copy in xcopies:
         copy.start()
-    signal(ready.at[0], z_peers[1])
-    signal(ready.at[0], z_peers[13])
+    for peer in beside:
+        signal(ready.at[0], peer)
     v1 = [
         remote(vmsg.at[(y + i) % 4], vnear.at[i - 1], sv1.at[i - 1], qv1.at[i - 1], y_peers[i - 1])
         for i in range(1, 4)
     ]
-    for copy in v1:
-        copy.start()
 
     where = (x, y)
     across = (x_peers, y_peers)
@@ -135,22 +130,27 @@
     first = [[], []]
     for l in range(2):
         xcopies[l].wait()
-        xcat[l, 128:256] = xrecv[l].astype(jnp.bfloat16)
-        corner = []
-        for i in range(4):
-            block = lax.dot_general(
-                xcat[l, :, 128 * i : 128 * i + 128],
-                xcat[l, :, 128 * i : 512],
-                (((0,), (0,)), ((), ())),
+        xcat[l, :, 128:256] = xrecv[l].astype(jnp.bfloat16)
+        right = [
+            lax.dot_general(
+                xcat[l, 0 : 256 + 256 * k],
+                xcat[l, 256 * k : 256 * k + 256],
+                (((1,), (1,)), ((), ())),
                 preferred_element_type=jnp.float32,
             )
-            corner.append(block[:, 0:128])
-            for j in range(i + 1, 4):
-                at = 256 + PAIRS.index((i, j)) * 128
-                terms[l, at : at + 128] = block[:, 128 * (j - i) : 128 * (j - i) + 128]
-        terms[l, 0:128] = jnp.where(at_or_above, corner[0], corner[1])
-        terms[l, 128:256] = jnp.where(at_or_above, corner[2], corner[3])
-        for i in range(1, 4):
+            for k in range(2)
+        ]
+
+        def pair(i, j):
+            return right[j // 2][128 * i : 128 * i + 128, 128 * (j % 2) : 128 * (j % 2) + 128]
+
+        terms[l, 0:128] = jnp.where(at_or_above, pair(0, 0), pair(1, 1))
+        terms[l, 128:256] = jnp.where(at_or_above, pair(2, 2), pair(3, 3))
+        for k, (i, j) in enumerate(PAIRS):
+            terms[l, 256 + 128 * k : 384 + 128 * k] = pair(i, j)
+        if l == 0:
+            pl.semaphore_wait(ready.at[0], len(beside))
+        for i in (2, 1, 3):
             to = (where[l] + i) % 4
             copy = remote(
                 terms.at[l, pl.ds(pl.multiple_of(to * 256, 256), 256)],
@@ -161,10 +161,15 @@
             )
             copy.start()
             first[l].append(copy)
-
-    pl.semaphore_wait(ready.at[0], 2)
-    signal(ready.at[1], z_peers[3])
-    signal(ready.at[1], z_peers[11])
+        if l == 0:
+            signal(ready.at[1], z_peers[1])
+            signal(ready.at[1], z_peers[13])
+            for i in (2, 1, 3):
+                v1[i - 1].start()
+
+    pl.semaphore_wait(ready.at[1], 2)
+    signal(ready.at[2], z_peers[3])
+    signal(ready.at[2], z_peers[11])
 
     for copy in v1:
         copy.wait()
@@ -185,7 +190,7 @@
         vboth[l, c] = vown[c, l, 0:16]
         vboth[l, 1 - c] = vcore[l, 0:16]
         diag_own[l] = vown[c, l, 16:18] + vcore[l, 16:18]
-    pl.semaphore_wait(ready.at[1], 2)
+    pl.semaphore_wait(ready.at[2], 2)
     far_first = (8, 7, 9, 6, 10, 5, 11, 4, 12, 3, 13, 2, 14, 1, 15)
     v3 = [
         remote(vboth.at[(z + i) % 2], vfar.at[i - 1], sv3.at[i - 1], qv3.at[i - 1], z_peers[i - 1])
@@ -215,7 +220,7 @@
             copy.wait()
         own = pl.ds(pl.multiple_of(where[l] * 256, 256), 256)
         chunk[l] = terms[l, own] + near[l, 0] + near[l, 1] + near[l, 2]
-        for i in range(1, 4):
+        for i in (2, 1, 3):
             to = (where[1 - l] + i) % 4
             copy = remote(
                 chunk.at[l, pl.ds(pl.multiple_of(to * 64, 64), 64)],
@@ -303,10 +308,19 @@
         fourth[i].start()
     mine = jnp.where(layer == 0, x * 4 + y, y * 4 + x)
     fifth = []
+    straight = []
+    for k in range(5):
+        i, j = plane_shift[k]
+        straight.append(
+            remote(
+                unit, stack.at[mine, 7], s5.at[45 + k], q5.at[45 + k], device((x + i) % 4, (y + j) % 4, (z + 8) % 16, c)
+            )
+        )
+        straight[k].start()
     for lo, hi in ((0, 3), (3, 7), (7, 8)):
         for i in NEAR_FIRST[max(lo, 1) - 1 : hi - 1]:
             fourth[i].wait_recv()
-        for k in range(15):
+        for k in range(5 if lo == 7 else 0, 15):
             at = len(fifth)
             fifth.append(
                 remote(zgath.at[lo:hi], stack.at[mine, lo:hi], s5.at[at], q5.at[at], plane_peers[k])
@@ -355,7 +369,7 @@
         copy.wait()
     second_diag = (diag_sum[...] + diag_x[0] + diag_x[1] + diag_x[2]) * scale
 
-    for copy in fifth:
+    for copy in fifth + straight:
         copy.wait()
     for i in NEAR_FIRST:
         fourth[i].wait_send()
@@ -412,7 +426,7 @@
     @pl.when(c == 1)
     def _():
         rcopy.wait_recv()
-        result = high(newrows[...], partner[...], (((1,), (1,)), ((), ())))
+        result = three(split(newrows[...]), split(partner[...]), (((1,), (1,)), ((), ())))
         for k in range(4):
             pblock[k] = result[16 * k : 16 * k + 16]
         pin[layer] = pblock[layer * 2 + 1]
@@ -445,6 +459,7 @@
     whole = pl.BlockSpec(memory_space=pltpu.VMEM)
     vm = lambda *shape: pltpu.VMEM(shape, f32)
     dma = lambda n: pltpu.SemaphoreType.DMA((n,))
+    operands = (owners, counts, activations, out_grads, inverse_slots, gradient)
     return pl.pallas_call(
         kernel,
         out_shape=(
@@ -459,9 +474,9 @@
             pltpu.VMEM((2, 2, 128, 512), bf16),
             vm(2, 2, 16, 512),
             vm(512, 512),
-            vm(2, 128, 512),
-            vm(2, 128, 512),
-            pltpu.VMEM((2, 256, 512), bf16),
+            vm(2, 512, 128),
+            vm(2, 512, 128),
+            pltpu.VMEM((2, 512, 256), bf16),
             vm(2, 1024, 128),
             vm(2, 3, 256, 128),
             vm(2, 256, 128),
@@ -496,15 +511,15 @@
             vm(2, 16, 32),
             vm(2, 2, 16, 512),
             dma(6), dma(2), dma(2), dma(6), dma(6), dma(6), dma(6), dma(15), dma(15), dma(7), dma(7),
-            dma(45), dma(45),
+            dma(50), dma(50),
             dma(3), dma(3), dma(1), dma(1), dma(15), dma(15), dma(45), dma(45), dma(15), dma(15), dma(3), dma(3),
             dma(3), dma(3), dma(1), dma(1), dma(3), dma(2),
-            pltpu.SemaphoreType.REGULAR((2,)),
+            pltpu.SemaphoreType.REGULAR((3,)),
         ],
         compiler_params=pltpu.CompilerParams(
-            collective_id=0, has_side_effects=True, vmem_limit_bytes=62 * 1024 * 1024
+            collective_id=0, has_side_effects=True, vmem_limit_bytes=40 * 1024 * 1024
         ),
-    )(owners, counts, activations, out_grads, inverse_slots, gradient)
+    )(*(pltpu.with_memory_space_constraint(a, pltpu.HBM) for a in operands))
 
 
 def solution(mesh):

time: 63.2 us -> 63.8 us (level)
  Pallas kernels: 59.4 us -> 61.7 us
  local copies, waits for them, and re-layouts: 2.89 us -> 1.26 us
    pallas_call x1, Pallas kernels: 59.4 us -> 61.7 us  [body(): pl.pallas_call(kernel, out_shape=(jax.ShapeDtypeStruct((2, 2, 16, 512), f...]
    unnamed x2, local copies, waits for them, and re-layouts: 2.89 us -> 1.26 us
where the time goes in v3:
time: 63.8 us; the launch traced here: 63.6 us
  Pallas kernels  61.7 us (97%)
  local copies, waits for them, and re-layouts  1.26 us (2%)
  between operations  0.64 us (1%)
    pallas_call x1, Pallas kernels, body(): pl.pallas_call(kernel, out_shape=(jax.ShapeDtypeStruct((2, 2, 16, 512), f...  61.7 us

profile of v3, /device:TPU:1, one launch (start us, length us, event | category | flops | bytes accessed | tf_op | source)
XLA Modules:
  0.0 63.6 jit_solution(12681479097470888593)
XLA Ops:
  0.6 61.7 %shard_map.77 = (f32[2,2,16,512]{3,2,1,0:T(8,128)S(1)}, f32[2,16,32]{2,1,0:T(8,128)S(1)}) custom-call(s32[2,2]{1,0:T(2,128)} %owners_in.1, s32[512]{0:T(512)} %counts_in.1, bf16[2,128,512]{2,1,0:T(8,128)(2,1)} %acts.1, bf16[2,128,512]{2,1,0:T(8,128)(2,1)} %grads.1, f32[2,2,16,512]{3,2,1,0:T(8,128)} %slots.1, f32[2,512,512]{2,1,0:T(8,128)} %gradient.1), custom_call_target="tpu_custom_call" | custom-call | tf_op jit(solution)/shard_map/pallas_call | solution.py:463
  62.4 0.7 %copy.10 = f32[2,2,16,512]{3,2,1,0:T(8,128)} copy(f32[2,2,16,512]{3,2,1,0:T(8,128)S(1)} %get-tuple-element.4) | data formatting | bytes 262144
  63.0 0.6 copy.11

commit v4 on v3

--- a/solution.py
+++ b/solution.py
@@ -25,10 +25,6 @@
 
 NEAR_FIRST = (2, 14, 4, 12, 6, 10, 8)
 PAIRS = ((0, 1), (0, 2), (0, 3), (1, 2), (1, 3), (2, 3))
-
-
-def in_half(a, b):
-    return (b - a) % 4 < 2 or ((b - a) % 4 == 2 and a < 2)
 
 
 def kernel(
@@ -72,8 +68,7 @@
     pair_peer = device(x, y, zpair, c)
     cross_peer = device(x, y, zpair, 1 - c)
     barrier = pltpu.get_barrier_semaphore()
-    beside = [x_peers[0], x_peers[2], y_peers[0], y_peers[2], z_peers[0], z_peers[14]]
-    close = [core_peer] + beside
+    close = [core_peer] + x_peers + y_peers + [z_peers[i - 1] for i in (1, 2, 14, 15)]
     for peer in close:
         signal(barrier, peer)
 
@@ -115,19 +110,23 @@
     xcopies = [remote(xsend.at[l], xrecv.at[l], xss.at[l], xrs.at[l], core_peer) for l in range(2)]
     for copy in xcopies:
         copy.start()
-    for peer in beside:
-        signal(ready.at[0], peer)
+    signal(ready.at[0], z_peers[1])
+    signal(ready.at[0], z_peers[13])
     v1 = [
         remote(vmsg.at[(y + i) % 4], vnear.at[i - 1], sv1.at[i - 1], qv1.at[i - 1], y_peers[i - 1])
         for i in range(1, 4)
     ]
 
+    for copy in v1:
+        copy.start()
     where = (x, y)
     across = (x_peers, y_peers)
     at_or_above = lax.broadcasted_iota(jnp.int32, (128, 128), 0) <= lax.broadcasted_iota(
         jnp.int32, (128, 128), 1
     )
-    first = [[], []]
+    turn_to = jnp.where(zlo < 2, 1, 3)
+    quads = [(zhi + 2) % 4, (zhi + turn_to) % 4, (zhi + 4 - turn_to) % 4, zhi]
+    first = [[[] for _ in range(4)] for _ in range(2)]
     for l in range(2):
         xcopies[l].wait()
         xcat[l, :, 128:256] = xrecv[l].astype(jnp.bfloat16)
@@ -144,32 +143,27 @@
         def pair(i, j):
             return right[j // 2][128 * i : 128 * i + 128, 128 * (j % 2) : 128 * (j % 2) + 128]
 
-        terms[l, 0:128] = jnp.where(at_or_above, pair(0, 0), pair(1, 1))
-        terms[l, 128:256] = jnp.where(at_or_above, pair(2, 2), pair(3, 3))
+        terms[l, 0, 0:2] = jnp.where(at_or_above, pair(0, 0), pair(1, 1)).reshape(2, 8, 8, 128)
+        terms[l, 0, 2:4] = jnp.where(at_or_above, pair(2, 2), pair(3, 3)).reshape(2, 8, 8, 128)
         for k, (i, j) in enumerate(PAIRS):
-            terms[l, 256 + 128 * k : 384 + 128 * k] = pair(i, j)
-        if l == 0:
-            pl.semaphore_wait(ready.at[0], len(beside))
-        for i in (2, 1, 3):
-            to = (where[l] + i) % 4
-            copy = remote(
-                terms.at[l, pl.ds(pl.multiple_of(to * 256, 256), 256)],
-                near.at[l, i - 1],
-                s1.at[l * 3 + i - 1],
-                q1.at[l * 3 + i - 1],
-                across[l][i - 1],
-            )
-            copy.start()
-            first[l].append(copy)
-        if l == 0:
-            signal(ready.at[1], z_peers[1])
-            signal(ready.at[1], z_peers[13])
+            b = k + 2
+            terms[l, b // 2, b % 2 * 2 : b % 2 * 2 + 2] = pair(i, j).reshape(2, 8, 8, 128)
+        for t in range(4):
             for i in (2, 1, 3):
-                v1[i - 1].start()
-
-    pl.semaphore_wait(ready.at[1], 2)
-    signal(ready.at[2], z_peers[3])
-    signal(ready.at[2], z_peers[11])
+                at = (l * 4 + t) * 3 + i - 1
+                copy = remote(
+                    terms.at[l, (where[l] + i) % 4, :, pl.ds(quads[t] * 2, 2)],
+                    near.at[l, t, i - 1],
+                    s1.at[at],
+                    q1.at[at],
+                    across[l][i - 1],
+                )
+                copy.start()
+                first[l][t].append(copy)
+
+    pl.semaphore_wait(ready.at[0], 2)
+    signal(ready.at[1], z_peers[3])
+    signal(ready.at[1], z_peers[11])
 
     for copy in v1:
         copy.wait()
@@ -190,7 +184,7 @@
         vboth[l, c] = vown[c, l, 0:16]
         vboth[l, 1 - c] = vcore[l, 0:16]
         diag_own[l] = vown[c, l, 16:18] + vcore[l, 16:18]
-    pl.semaphore_wait(ready.at[2], 2)
+    pl.semaphore_wait(ready.at[1], 2)
     far_first = (8, 7, 9, 6, 10, 5, 11, 4, 12, 3, 13, 2, 14, 1, 15)
     v3 = [
         remote(vboth.at[(z + i) % 2], vfar.at[i - 1], sv3.at[i - 1], qv3.at[i - 1], z_peers[i - 1])
@@ -201,58 +195,76 @@
         for i in range(1, 16)
     ]
 
-    def kept(step):
+    def kept(step, side):
         row = (zlo + 4 - step) % 4
         turn = (y - row + 4) % 4
-        return (turn < 2) | ((turn == 2) & (row < 2))
-
-    @pl.when(kept(0))
-    def _():
-        for i in far_first:
-            v3[i - 1].start()
+        return (turn < 2) | ((turn == 2) & (row // 2 == side))
+
+    for odd in range(2):
+
+        @pl.when(kept(0, (layer + odd) % 2))
+        def _():
+            for i in far_first:
+                if i % 2 == odd:
+                    v3[i - 1].start()
 
     for i in far_first:
         e3[i - 1].start()
 
-    second = [[], []]
-    for l in range(2):
-        for copy in first[l]:
-            copy.wait()
-        own = pl.ds(pl.multiple_of(where[l] * 256, 256), 256)
-        chunk[l] = terms[l, own] + near[l, 0] + near[l, 1] + near[l, 2]
-        for i in (2, 1, 3):
-            to = (where[1 - l] + i) % 4
-            copy = remote(
-                chunk.at[l, pl.ds(pl.multiple_of(to * 64, 64), 64)],
-                near2.at[l, i - 1],
-                s2.at[l * 3 + i - 1],
-                q2.at[l * 3 + i - 1],
-                across[1 - l][i - 1],
+    second = [[[] for _ in range(4)] for _ in range(2)]
+
+    def to_second(t):
+        for l in range(2):
+            for copy in first[l][t]:
+                copy.wait()
+            chunk[l, t] = (
+                terms[l, where[l], :, pl.ds(quads[t] * 2, 2)] + near[l, t, 0] + near[l, t, 1] + near[l, t, 2]
             )
-            copy.start()
-            second[l].append(copy)
-    for l in range(2):
-        for copy in second[l]:
-            copy.wait()
-        own = pl.ds(pl.multiple_of(where[1 - l] * 64, 64), 64)
-        part[l] = (chunk[l, own] + near2[l, 0] + near2[l, 1] + near2[l, 2]).reshape(8, 8, 128)
-    third = [
-        remote(
-            part.at[(z + i) % 2, (z + i) % 16 // 2], zrecv.at[i - 1], s3.at[i - 1], q3.at[i - 1], z_peers[i - 1]
-        )
-        for i in range(1, 16)
-    ]
-    for i in far_first:
-        third[i - 1].start()
-
-    @pl.when(kept(0))
-    def _():
-        for copy in v3:
-            copy.wait_send()
+            for i in (2, 1, 3):
+                at = (l * 4 + t) * 3 + i - 1
+                copy = remote(
+                    chunk.at[l, t, (where[1 - l] + i) % 4],
+                    near2.at[l, t, i - 1],
+                    s2.at[at],
+                    q2.at[at],
+                    across[1 - l][i - 1],
+                )
+                copy.start()
+                second[l][t].append(copy)
+
+    def to_planes(t):
+        for l in range(2):
+            for copy in second[l][t]:
+                copy.wait()
+            part[l, t] = chunk[l, t, where[1 - l]] + near2[l, t, 0] + near2[l, t, 1] + near2[l, t, 2]
+        for r in range(1 if t == 3 else 0, 4):
+            lane = (zlo + r) % 4
+            target = quads[t] * 4 + lane
+            at = (target + 16 - z) % 16 - 1
+            remote(
+                part.at[lane % 2, t, lane // 2], zrecv.at[at], s3.at[at], q3.at[at], device(x, y, target, c)
+            ).start()
+
+    to_second(0)
+    to_second(1)
+    to_planes(0)
+    to_second(2)
+    to_planes(1)
+    to_second(3)
+    to_planes(2)
+    to_planes(3)
+
+    for odd in range(2):
+
+        @pl.when(kept(0, (layer + odd) % 2))
+        def _():
+            for i in range(1, 16):
+                if i % 2 == odd:
+                    v3[i - 1].wait_send()
 
     for r in range(4):
 
-        @pl.when(kept(r))
+        @pl.when(kept(r, layer))
         def _():
             got = vboth[layer] if r == 0 else None
             for i in range(r or 4, 16, 4):
@@ -277,7 +289,7 @@
         for copy in v4[d]:
             copy.start()
 
-    @pl.when(y >= 2)
+    @pl.when((y // 2 + layer) % 2 == 1)
     def _():
         row = (y + 2) % 4
         vcols[y, row, x] = vpart[row]
@@ -293,9 +305,9 @@
     for copy in e4:
         copy.start()
 
-    for copy in third:
-        copy.wait()
-    got = part[layer, z // 2]
+    for i in range(15):
+        remote(part.at[0, 0, 0], zrecv.at[i], s3.at[i], q3.at[i], z_peers[i]).wait()
+    got = part[layer, 3, zlo // 2]
     for i in range(15):
         got = got + zrecv[i]
     unit[...] = got * scale
@@ -313,11 +325,11 @@
         i, j = plane_shift[k]
         straight.append(
             remote(
-                unit, stack.at[mine, 7], s5.at[45 + k], q5.at[45 + k], device((x + i) % 4, (y + j) % 4, (z + 8) % 16, c)
+                unit, stack.at[mine, 7], s5.at[70 + k], q5.at[70 + k], device((x + i) % 4, (y + j) % 4, (z + 8) % 16, c)
             )
         )
         straight[k].start()
-    for lo, hi in ((0, 3), (3, 7), (7, 8)):
+    for lo, hi in ((0, 1), (1, 3), (3, 5), (5, 7), (7, 8)):
         for i in NEAR_FIRST[max(lo, 1) - 1 : hi - 1]:
             fourth[i].wait_recv()
         for k in range(5 if lo == 7 else 0, 15):
@@ -332,18 +344,26 @@
         v4[0][k].wait()
         v4[1][k].wait()
 
-        @pl.when((y + 4 - j) % 4 >= 2)
+        @pl.when(((y + 4 - j) % 4 // 2 + layer) % 2 == 1)
         def _():
             v4[2][k].wait_recv()
 
-        @pl.when(y >= 2)
+        @pl.when((y // 2 + layer) % 2 == 1)
         def _():
             v4[2][k].wait_send()
 
     for a in range(4):
-        for b in range(4):
-            block = vcols[b, a].reshape(128, 128) if in_half(a, b) else vcols[a, b].reshape(128, 128).T
+        for b in (a, (a + 1) % 4):
+            block = vcols[b, a].reshape(128, 128)
             vfull[128 * a : 128 * a + 128, 128 * b : 128 * b + 128] = block
+            if a != b:
+                vfull[128 * b : 128 * b + 128, 128 * a : 128 * a + 128] = block.T
+    for a in range(2):
+        b = a + 2
+        block = vcols[a + 2 * (1 - layer), a + 2 * layer].reshape(128, 128)
+        turned = block.T
+        vfull[128 * a : 128 * a + 128, 128 * b : 128 * b + 128] = jnp.where(layer == 0, block, turned)
+        vfull[128 * b : 128 * b + 128, 128 * a : 128 * a + 128] = jnp.where(layer == 0, turned, block)
     row_a = jnp.where(c == 1, (zlo // 2 * 2) * 4 + x, y * 4 + zhi)
     row_b = jnp.where(c == 1, (zlo // 2 * 2 + 1) * 4 + x, y * 4 + zhi)
     rows_in[0:32] = vfull[pl.ds(pl.multiple_of(row_a * 32, 32), 32)]
@@ -477,11 +497,11 @@
             vm(2, 512, 128),
             vm(2, 512, 128),
             pltpu.VMEM((2, 512, 256), bf16),
-            vm(2, 1024, 128),
-            vm(2, 3, 256, 128),
-            vm(2, 256, 128),
-            vm(2, 3, 64, 128),
-            vm(2, 8, 8, 128),
+            vm(2, 4, 4, 8, 8, 128),
+            vm(2, 4, 3, 4, 2, 8, 128),
+            vm(2, 4, 4, 2, 8, 128),
+            vm(2, 4, 3, 2, 8, 128),
+            vm(2, 4, 2, 8, 128),
             vm(15, 8, 128),
             vm(8, 128),
             vm(8, 8, 128),
@@ -510,11 +530,11 @@
             vm(4, 16, 32),
             vm(2, 16, 32),
             vm(2, 2, 16, 512),
-            dma(6), dma(2), dma(2), dma(6), dma(6), dma(6), dma(6), dma(15), dma(15), dma(7), dma(7),
-            dma(50), dma(50),
+            dma(6), dma(2), dma(2), dma(24), dma(24), dma(24), dma(24), dma(15), dma(15), dma(7), dma(7),
+            dma(75), dma(75),
             dma(3), dma(3), dma(1), dma(1), dma(15), dma(15), dma(45), dma(45), dma(15), dma(15), dma(3), dma(3),
             dma(3), dma(3), dma(1), dma(1), dma(3), dma(2),
-            pltpu.SemaphoreType.REGULAR((3,)),
+            pltpu.SemaphoreType.REGULAR((2,)),
         ],
         compiler_params=pltpu.CompilerParams(
             collective_id=0, has_side_effects=True, vmem_limit_bytes=40 * 1024 * 1024

time: 63.8 us -> 60.8 us (0.953)
  Pallas kernels: 61.7 us -> 58.8 us
    pallas_call x1, Pallas kernels: 61.7 us -> 58.8 us  [body(): pl.pallas_call(kernel, out_shape=(jax.ShapeDtypeStruct((2, 2, 16, 512), f...]
where the time goes in v4:
time: 60.8 us; the launch traced here: 60.7 us
  Pallas kernels  58.8 us (97%)
  local copies, waits for them, and re-layouts  1.26 us (2%)
  between operations  0.64 us (1%)
    pallas_call x1, Pallas kernels, body(): pl.pallas_call(kernel, out_shape=(jax.ShapeDtypeStruct((2, 2, 16, 512), f...  58.8 us
    unnamed x2, local copies, waits for them, and re-layouts  1.26 us

profile of v4, /device:TPU:1, one launch (start us, length us, event | category | flops | bytes accessed | tf_op | source)
XLA Modules:
  0.0 60.7 jit_solution(10174906792247056718)
XLA Ops:
  0.6 58.8 %shard_map.77 = (f32[2,2,16,512]{3,2,1,0:T(8,128)S(1)}, f32[2,16,32]{2,1,0:T(8,128)S(1)}) custom-call(s32[2,2]{1,0:T(2,128)} %owners_in.1, s32[512]{0:T(512)} %counts_in.1, bf16[2,128,512]{2,1,0:T(8,128)(2,1)} %acts.1, bf16[2,128,512]{2,1,0:T(8,128)(2,1)} %grads.1, f32[2,2,16,512]{3,2,1,0:T(8,128)} %slots.1, f32[2,512,512]{2,1,0:T(8,128)} %gradient.1), custom_call_target="tpu_custom_call" | custom-call | tf_op jit(solution)/shard_map/pallas_call | solution.py:483
  59.4 0.7 %copy.10 = f32[2,2,16,512]{3,2,1,0:T(8,128)} copy(f32[2,2,16,512]{3,2,1,0:T(8,128)S(1)} %get-tuple-element.4) | data formatting | bytes 262144
  60.1 0.6 copy.11

commit v5 on v4

--- a/solution.py
+++ b/solution.py
@@ -195,17 +195,18 @@
         for i in range(1, 16)
     ]
 
-    def kept(step, side):
+    def kept(step, side, column=y):
         row = (zlo + 4 - step) % 4
-        turn = (y - row + 4) % 4
+        turn = (column - row + 4) % 4
         return (turn < 2) | ((turn == 2) & (row // 2 == side))
 
-    for odd in range(2):
-
-        @pl.when(kept(0, (layer + odd) % 2))
+    steps = (0, 1, 3, 2)
+    for r in steps:
+
+        @pl.when(kept(0, (layer + r) % 2))
         def _():
             for i in far_first:
-                if i % 2 == odd:
+                if i % 4 == r:
                     v3[i - 1].start()
 
     for i in far_first:
@@ -254,15 +255,20 @@
     to_planes(2)
     to_planes(3)
 
-    for odd in range(2):
-
-        @pl.when(kept(0, (layer + odd) % 2))
-        def _():
-            for i in range(1, 16):
-                if i % 2 == odd:
-                    v3[i - 1].wait_send()
-
-    for r in range(4):
+    v4 = [
+        [
+            remote(
+                vpart.at[(zlo + 4 - r) % 4],
+                vcols.at[y, (zlo + 4 - r) % 4, x],
+                sv4.at[r * 15 + k],
+                qv4.at[r * 15 + k],
+                plane_peers[k],
+            )
+            for k in range(15)
+        ]
+        for r in range(4)
+    ]
+    for r in steps:
 
         @pl.when(kept(r, layer))
         def _():
@@ -270,31 +276,19 @@
             for i in range(r or 4, 16, 4):
                 v3[i - 1].wait_recv()
                 got = vfar[i - 1] if got is None else got + vfar[i - 1]
-            vpart[(zlo + 4 - r) % 4] = got
-
-    v4 = []
-    for d in range(3):
-        row = (y + 4 - d) % 4
-        v4.append(
-            [
-                remote(
-                    vpart.at[row], vcols.at[y, row, x], sv4.at[d * 15 + k], qv4.at[d * 15 + k], plane_peers[k]
-                )
-                for k in range(15)
-            ]
-        )
-    for d in range(2):
-        row = (y + 4 - d) % 4
-        vcols[y, row, x] = vpart[row]
-        for copy in v4[d]:
-            copy.start()
-
-    @pl.when((y // 2 + layer) % 2 == 1)
-    def _():
-        row = (y + 2) % 4
-        vcols[y, row, x] = vpart[row]
-        for copy in v4[2]:
-            copy.start()
+            row = (zlo + 4 - r) % 4
+            vpart[row] = got
+            vcols[y, row, x] = got
+            for copy in v4[r]:
+                copy.start()
+
+    for odd in range(2):
+
+        @pl.when(kept(0, (layer + odd) % 2))
+        def _():
+            for i in range(1, 16):
+                if i % 2 == odd:
+                    v3[i - 1].wait_send()
 
     got = diag_own[layer]
     for i in range(15):
@@ -340,17 +334,19 @@
             fifth[at].start()
     stack[mine] = zgath[...]
 
-    for k, (i, j) in enumerate(plane_shift):
-        v4[0][k].wait()
-        v4[1][k].wait()
-
-        @pl.when(((y + 4 - j) % 4 // 2 + layer) % 2 == 1)
+    for r in range(4):
+        for back in range(4):
+
+            @pl.when(kept(r, layer, (y + 4 - back) % 4))
+            def _():
+                for k, (i, j) in enumerate(plane_shift):
+                    if j == back:
+                        v4[r][k].wait_recv()
+
+        @pl.when(kept(r, layer))
         def _():
-            v4[2][k].wait_recv()
-
-        @pl.when((y // 2 + layer) % 2 == 1)
-        def _():
-            v4[2][k].wait_send()
+            for copy in v4[r]:
+                copy.wait_send()
 
     for a in range(4):
         for b in (a, (a + 1) % 4):
@@ -532,7 +528,7 @@
             vm(2, 2, 16, 512),
             dma(6), dma(2), dma(2), dma(24), dma(24), dma(24), dma(24), dma(15), dma(15), dma(7), dma(7),
             dma(75), dma(75),
-            dma(3), dma(3), dma(1), dma(1), dma(15), dma(15), dma(45), dma(45), dma(15), dma(15), dma(3), dma(3),
+            dma(3), dma(3), dma(1), dma(1), dma(15), dma(15), dma(60), dma(60), dma(15), dma(15), dma(3), dma(3),
             dma(3), dma(3), dma(1), dma(1), dma(3), dma(2),
             pltpu.SemaphoreType.REGULAR((2,)),
         ],

time: 60.8 us -> 59.4 us (0.977)
  Pallas kernels: 58.8 us -> 57.4 us
    pallas_call x1, Pallas kernels: 58.8 us -> 57.4 us  [body(): pl.pallas_call(kernel, out_shape=(jax.ShapeDtypeStruct((2, 2, 16, 512), f...]
where the time goes in v5:
time: 59.4 us; the launch traced here: 59.3 us
  Pallas kernels  57.4 us (97%)
  local copies, waits for them, and re-layouts  1.26 us (2%)
  between operations  0.64 us (1%)
    pallas_call x1, Pallas kernels, body(): pl.pallas_call(kernel, out_shape=(jax.ShapeDtypeStruct((2, 2, 16, 512), f...  57.4 us
    unnamed x2, local copies, waits for them, and re-layouts  1.26 us

profile of v5, /device:TPU:1, one launch (start us, length us, event | category | flops | bytes accessed | tf_op | source)
XLA Modules:
  0.0 59.3 jit_solution(7618539336178323363)
XLA Ops:
  0.6 57.4 %shard_map.77 = (f32[2,2,16,512]{3,2,1,0:T(8,128)S(1)}, f32[2,16,32]{2,1,0:T(8,128)S(1)}) custom-call(s32[2,2]{1,0:T(2,128)} %owners_in.1, s32[512]{0:T(512)} %counts_in.1, bf16[2,128,512]{2,1,0:T(8,128)(2,1)} %acts.1, bf16[2,128,512]{2,1,0:T(8,128)(2,1)} %grads.1, f32[2,2,16,512]{3,2,1,0:T(8,128)} %slots.1, f32[2,512,512]{2,1,0:T(8,128)} %gradient.1), custom_call_target="tpu_custom_call" | custom-call | tf_op jit(solution)/shard_map/pallas_call | solution.py:479
  58.0 0.7 %copy.10 = f32[2,2,16,512]{3,2,1,0:T(8,128)} copy(f32[2,2,16,512]{3,2,1,0:T(8,128)S(1)} %get-tuple-element.4) | data formatting | bytes 262144
  58.7 0.6 %copy.11 = f32[2,16,32]{2,1,0:T(8,128)} copy(f32[2,16,32]{2,1,0:T(8,128)S(1)} %get-tuple-element.5) | data formatting | bytes 8192

commit v6 on v5

--- a/solution.py
+++ b/solution.py
@@ -160,10 +160,10 @@
                 )
                 copy.start()
                 first[l][t].append(copy)
-
-    pl.semaphore_wait(ready.at[0], 2)
-    signal(ready.at[1], z_peers[3])
-    signal(ready.at[1], z_peers[11])
+        if l == 0:
+            pl.semaphore_wait(ready.at[0], 2)
+            signal(ready.at[1], z_peers[3])
+            signal(ready.at[1], z_peers[11])
 
     for copy in v1:
         copy.wait()

time: 59.4 us -> 58.9 us (level)
  no operation moved by 1% of the time
where the time goes in v6:
time: 58.9 us; the launch traced here: 58.8 us
  Pallas kernels  56.9 us (97%)
  local copies, waits for them, and re-layouts  1.26 us (2%)
  between operations  0.64 us (1%)
    pallas_call x1, Pallas kernels, body(): pl.pallas_call(kernel, out_shape=(jax.ShapeDtypeStruct((2, 2, 16, 512), f...  56.9 us
    unnamed x2, local copies, waits for them, and re-layouts  1.26 us

profile of v6, /device:TPU:1, one launch (start us, length us, event | category | flops | bytes accessed | tf_op | source)
XLA Modules:
  0.0 58.8 jit_solution(16617138084333760447)
XLA Ops:
  0.6 56.9 %shard_map.77 = (f32[2,2,16,512]{3,2,1,0:T(8,128)S(1)}, f32[2,16,32]{2,1,0:T(8,128)S(1)}) custom-call(s32[2,2]{1,0:T(2,128)} %owners_in.1, s32[512]{0:T(512)} %counts_in.1, bf16[2,128,512]{2,1,0:T(8,128)(2,1)} %acts.1, bf16[2,128,512]{2,1,0:T(8,128)(2,1)} %grads.1, f32[2,2,16,512]{3,2,1,0:T(8,128)} %slots.1, f32[2,512,512]{2,1,0:T(8,128)} %gradient.1), custom_call_target="tpu_custom_call" | custom-call | tf_op jit(solution)/shard_map/pallas_call | solution.py:479
  57.5 0.7 %copy.10 = f32[2,2,16,512]{3,2,1,0:T(8,128)} copy(f32[2,2,16,512]{3,2,1,0:T(8,128)S(1)} %get-tuple-element.4) | data formatting | bytes 262144
  58.2 0.6 %copy.11 = f32[2,16,32]{2,1,0:T(8,128)} copy(f32[2,16,32]{2,1,0:T(8,128)S(1)} %get-tuple-element.5) | data formatting | bytes 8192
